TPU v7x, 512 devices: a whole 4x8x8 slice. The times are simulated.
512 devices in a mesh: dp: 16 (over x_lo, z), tensor: 32 (over x_hi, y, core).
Axes of the slice: x: 4 (x_hi: 2, x_lo: 2; x = x_hi * 2 + x_lo), y: 8, z: 8, core: 2. Of those that a mesh axis runs over, the one named last changes fastest.
Arguments:
- activations: bfloat16 [2048, 28672], P('dp', 'tensor'), may hold values from -6 to 6
- cotangent: bfloat16 [2048, 8192], P('dp'), may hold values from -6 to 6
- weight: bfloat16 [28672, 8192], P('tensor', 'dp'), may hold values from -0.0625 to 0.0625
- clip_mask: int32 [2048, 28672], P('dp', 'tensor'), may hold values 0 or 1
- scale_exponent: int32 [2048], P('dp'), may hold values from -3 to 0
Outputs:
- input_gradient: bfloat16 [2048, 28672], P('dp', 'tensor')
- weight_gradient: bfloat16 [28672, 8192], P('tensor', 'dp')
All inputs are finite; a program needn't handle non-finite values. No bound on the sum of `clip_mask` on one device may be relied on, other than what follows from the above.
Results may differ from a plain program's by a relative error of at most 0.027.
Values may be sent and summed in bfloat16 or wider, within the bound.
A program may use at most 64 MiB of HBM per device.

v0:
```python
import math

import jax
import jax.numpy as jnp
import numpy as np
from jax import lax
from jax.sharding import PartitionSpec as P

FF = 28672


def swapped(value, axis, apart):
    mask = 2**apart
    pairs = [(source, source ^ mask) for source in range(lax.axis_size(axis))]
    return lax.ppermute(value, axis, pairs)


def paley_table():
    residues = set((number * number % 13 for number in range(1, 13)))
    jacobi = np.zeros((13, 13))
    for row_at in range(13):
        for col_at in range(13):
            differ = (col_at - row_at) % 13
            if differ != 0:
                jacobi[row_at, col_at] = 1.0 if differ in residues else -1.0
    confer = np.zeros((14, 14))
    confer[0, 1:] = 1.0
    confer[1:, 0] = 1.0
    confer[1:, 1:] = jacobi
    return np.kron(confer, np.array([[1.0, 1.0], [1.0, -1.0]])) + np.kron(
        np.eye(14), np.array([[1.0, -1.0], [-1.0, -1.0]])
    )


def sylvester(points):
    counter = jnp.arange(points, dtype=jnp.int32)
    common = jnp.bitwise_and(counter[:, None], counter[None, :])
    parity = jnp.zeros((points, points), jnp.int32)
    for bit_pos in range(points.bit_length() - 1):
        parity = parity + jnp.bitwise_and(jnp.right_shift(common, bit_pos), 1)
    return (1 - 2 * (parity % 2)).astype(jnp.float32)


def spread_devices(values):
    device_count = lax.axis_size("tensor")
    position = lax.axis_index("tensor")
    for bit_pos in range(device_count.bit_length() - 1):
        partner = swapped(values.astype(jnp.bfloat16), "tensor", bit_pos).astype(values.dtype)
        upper_half = jnp.bitwise_and(jnp.right_shift(position, bit_pos), 1) == 1
        values = jnp.where(upper_half, partner - values, values + partner)
    return values


def body(activations, cotangent, weight, clip_mask, scale_exponent):
    tok_rows, shard_width = activations.shape
    group_rows = shard_width // 28
    kron_table = jnp.kron(sylvester(group_rows), jnp.asarray(paley_table(), jnp.float32)).astype(
        jnp.bfloat16
    )
    normal_factor = 1.0 / math.sqrt(FF)
    local_rot = jnp.dot(activations, kron_table, preferred_element_type=jnp.float32)
    rotated = spread_devices(local_rot) * normal_factor
    step_size = jnp.exp2(scale_exponent.astype(jnp.float32))[:, None]
    quantized = jnp.clip(rotated, -8.0 * step_size, 7.0 * step_size).astype(jnp.bfloat16)
    swapped_grad = lax.all_to_all(cotangent, "dp", split_axis=1, concat_axis=0, tiled=True)
    token_total = swapped_grad.shape[0]
    grad_in = lax.psum_scatter(
        lax.dot_general(
            swapped_grad, weight, (((1,), (1,)), ((), ())), preferred_element_type=jnp.float32
        ).astype(jnp.bfloat16),
        "dp",
        scatter_dimension=0,
        tiled=True,
    ).astype(jnp.float32)
    masked = (clip_mask.astype(jnp.float32) * grad_in).astype(jnp.bfloat16)
    back_local = jnp.dot(masked, kron_table.T, preferred_element_type=jnp.float32)
    input_gradient = (spread_devices(back_local) * normal_factor).astype(jnp.bfloat16)
    zero_total = jnp.zeros((shard_width, swapped_grad.shape[1]), jnp.float32)
    shard_rows = lax.all_gather(quantized, "dp", axis=0, tiled=True)
    grad_rows = lax.slice_in_dim(swapped_grad, 0, shard_rows.shape[0], axis=0)
    summed = zero_total + lax.dot_general(
        shard_rows, grad_rows, (((0,), (0,)), ((), ())), preferred_element_type=jnp.float32
    )
    weight_gradient = (summed * (1.0 / math.sqrt(token_total))).astype(jnp.bfloat16)
    return (input_gradient, weight_gradient)


def solution(mesh):
    return jax.shard_map(
        body,
        mesh=mesh,
        in_specs=(P("dp", "tensor"), P("dp", None), P("tensor", "dp"), P("dp", "tensor"), P("dp")),
        out_specs=(P("dp", "tensor"), P("tensor", "dp")),
        check_vma=False,
    )
```

profile of v0, /device:TPU:12, one launch (start us, length us, event | category | flops | bytes accessed | tf_op | source)
XLA Modules:
  0.0 252.6 jit_solution(10159328632294804262)
XLA Ops:
  7.2 4.1 %copy.10 = bf16[128,8192]{0,1:T(8,128)(2,1)} copy(bf16[128,8192]{1,0:T(8,128)(2,1)} %param.7) | data formatting | bytes 4194304 | tf_op args[1]
  11.4 60.5 %all_to_all.19 = bf16[128,16,512]{0,2,1:T(8,128)(2,1)S(1)} all-to-all(bf16[128,16,512]{0,2,1:T(8,128)(2,1)} %bitcast.15), channel_id=1, replica_groups=mesh['dp'=16,'tensor'=32] {'dp'}, dimensions={1} | all-to-all | bytes 4194304 | tf_op jit(solution)/shard_map/all_to_all | solution.py:65
  71.8 2.6 %copy.11 = bf16[16,128,512]{2,1,0:T(8,128)(2,1)} copy(bf16[16,128,512]{1,2,0:T(8,128)(2,1)S(1)} %bitcast.14) | data formatting | bytes 4194304 | tf_op jit(solution)/shard_map/all_to_all | solution.py:65
  74.5 5.9 %convolution_convert_fusion = bf16[2048,896]{1,0:T(8,128)(2,1)} fusion(bf16[2048,512]{1,0:T(8,128)(2,1)} %bitcast.16, bf16[896,512]{1,0:T(8,128)(2,1)S(1)} %copy-done), kind=kOutput, calls=%fused_computation.1 | convolution fusion | flops 1880883200 | bytes 6684672 | tf_op jit(solution)/shard_map/dot_general | solution.py:68
  81.1 4.7 %multiply_convert_fusion = bf16[32,28,32,28]{3,2,1,0:T(8,128)(2,1)} fusion(f32[28,28]{1,0:T(8,128)S(1)} %copy-done.7, f32[32,32]{1,0:T(8,128)S(1)} %fusion.26), kind=kLoop, calls=%fused_computation | loop fusion | flops 1605632 | bytes 1612864 | tf_op jit(solution)/shard_map/convert_element_type | solution.py:57
  85.8 13.6 %convert_element_type.103 = bf16[896,896]{1,0:T(8,128)(2,1)S(1)} reshape(bf16[32,28,32,28]{3,2,1,0:T(8,128)(2,1)} %multiply_convert_fusion) | data formatting | bytes 3211264 | tf_op jit(solution)/shard_map/convert_element_type | solution.py:57
  99.9 1.9 collective-permute-start.5
  101.8 1.4 collective-permute-done.5
  104.0 2.5 collective-permute-start.6
  106.5 7.4 %collective-permute-done.6 = bf16[128,896]{1,0:T(8,128)(2,1)S(1)} collective-permute-done((bf16[128,896]{1,0:T(8,128)(2,1)}, bf16[128,896]{1,0:T(8,128)(2,1)S(1)}, u32[]{:S(2)}, u32[]{:S(2)}) %collective-permute-start.6) | collective-permute-done | bytes 229408 | tf_op jit(solution)/shard_map/ppermute | solution.py:15
  114.7 4.5 %collective-permute-start.7 = (bf16[128,896]{1,0:T(8,128)(2,1)}, bf16[128,896]{1,0:T(8,128)(2,1)}, u32[]{:S(2)}, u32[]{:S(2)}) collective-permute-start(bf16[128,896]{1,0:T(8,128)(2,1)} %fusion.17), channel_id=1, source_target_pairs={{0,4},{1,5},{2,6},{3,7},{4,0},{5,1},{6,2},{7,3},{8,12},{9,13},{10,... | collective-permute-start | bytes 688136 | tf_op jit(solution)/shard_map/ppermute | solution.py:15
  119.2 9.4 %collective-permute-done.7 = bf16[128,896]{1,0:T(8,128)(2,1)} collective-permute-done((bf16[128,896]{1,0:T(8,128)(2,1)}, bf16[128,896]{1,0:T(8,128)(2,1)}, u32[]{:S(2)}, u32[]{:S(2)}) %collective-permute-start.7) | collective-permute-done | bytes 229408 | tf_op jit(solution)/shard_map/ppermute | solution.py:15
  128.7 2.0 fusion.27
  130.7 5.1 %collective-permute-start.8 = (bf16[128,896]{1,0:T(8,128)(2,1)}, bf16[128,896]{1,0:T(8,128)(2,1)S(1)}, u32[]{:S(2)}, u32[]{:S(2)}) collective-permute-start(bf16[128,896]{1,0:T(8,128)(2,1)} %get-tuple-element.2), channel_id=1, source_target_pairs={{0,8},{1,9},{2,10},{3,11},{4,12},{5,13},{6,14},{7,15},{8,0},{9,1},... | collective-permute-start | bytes 688136 | tf_op jit(solution)/shard_map/ppermute | solution.py:15
  135.8 8.8 %collective-permute-done.8 = bf16[128,896]{1,0:T(8,128)(2,1)S(1)} collective-permute-done((bf16[128,896]{1,0:T(8,128)(2,1)}, bf16[128,896]{1,0:T(8,128)(2,1)S(1)}, u32[]{:S(2)}, u32[]{:S(2)}) %collective-permute-start.8) | collective-permute-done | bytes 229408 | tf_op jit(solution)/shard_map/ppermute | solution.py:15
  144.7 2.8 %collective-permute-start.9 = (bf16[128,896]{1,0:T(8,128)(2,1)S(1)}, bf16[128,896]{1,0:T(8,128)(2,1)}, u32[]{:S(2)}, u32[]{:S(2)}) collective-permute-start(bf16[128,896]{1,0:T(8,128)(2,1)S(1)} %fusion.16), channel_id=1, source_target_pairs={{0,16},{1,17},{2,18},{3,19},{4,20},{5,21},{6,22},{7,23},{8,24},{9,... | collective-permute-start | bytes 688136 | tf_op jit(solution)/shard_map/ppermute | solution.py:15
  147.6 8.8 %collective-permute-done.9 = bf16[128,896]{1,0:T(8,128)(2,1)} collective-permute-done((bf16[128,896]{1,0:T(8,128)(2,1)S(1)}, bf16[128,896]{1,0:T(8,128)(2,1)}, u32[]{:S(2)}, u32[]{:S(2)}) %collective-permute-start.9) | collective-permute-done | bytes 229408 | tf_op jit(solution)/shard_map/ppermute | solution.py:15
  156.4 1.8 fusion.15
  158.3 2.4 reduce-scatter.2.cloned.1.call-done
  160.7 1.7 fusion.31
  162.5 1.9 collective-permute-start
  164.4 1.5 collective-permute-done
  165.9 4.3 %collective-permute-start.1 = (bf16[128,896]{1,0:T(8,128)(2,1)S(1)}, bf16[128,896]{1,0:T(8,128)(2,1)S(1)}, u32[]{:S(2)}, u32[]{:S(2)}) collective-permute-start(bf16[128,896]{1,0:T(8,128)(2,1)S(1)} %fusion.22), channel_id=1, source_target_pairs={{0,2},{1,3},{2,0},{3,1},{4,6},{5,7},{6,4},{7,5},{8,10},{9,11},{10,... | collective-permute-start | bytes 688136 | tf_op jit(solution)/shard_map/ppermute | solution.py:15
  170.3 5.9 %collective-permute-done.1 = bf16[128,896]{1,0:T(8,128)(2,1)S(1)} collective-permute-done((bf16[128,896]{1,0:T(8,128)(2,1)S(1)}, bf16[128,896]{1,0:T(8,128)(2,1)S(1)}, u32[]{:S(2)}, u32[]{:S(2)}) %collective-permute-start.1) | collective-permute-done | bytes 229408 | tf_op jit(solution)/shard_map/ppermute | solution.py:15
  176.3 6.3 %collective-permute-start.2 = (bf16[128,896]{1,0:T(8,128)(2,1)S(1)}, bf16[128,896]{1,0:T(8,128)(2,1)S(1)}, u32[]{:S(2)}, u32[]{:S(2)}) collective-permute-start(bf16[128,896]{1,0:T(8,128)(2,1)S(1)} %fusion.19), channel_id=1, source_target_pairs={{0,4},{1,5},{2,6},{3,7},{4,0},{5,1},{6,2},{7,3},{8,12},{9,13},{10,... | collective-permute-start | bytes 688136 | tf_op jit(solution)/shard_map/ppermute | solution.py:15
  182.6 9.3 %collective-permute-done.2 = bf16[128,896]{1,0:T(8,128)(2,1)S(1)} collective-permute-done((bf16[128,896]{1,0:T(8,128)(2,1)S(1)}, bf16[128,896]{1,0:T(8,128)(2,1)S(1)}, u32[]{:S(2)}, u32[]{:S(2)}) %collective-permute-start.2) | collective-permute-done | bytes 229408 | tf_op jit(solution)/shard_map/ppermute | solution.py:15
  192.1 5.0 %collective-permute-start.3 = (bf16[128,896]{1,0:T(8,128)(2,1)S(1)}, bf16[128,896]{1,0:T(8,128)(2,1)S(1)}, u32[]{:S(2)}, u32[]{:S(2)}) collective-permute-start(bf16[128,896]{1,0:T(8,128)(2,1)S(1)} %get-tuple-element.4), channel_id=1, source_target_pairs={{0,8},{1,9},{2,10},{3,11},{4,12},{5,13},{6,14},{7,15},{8,0},{9,1},... | collective-permute-start | bytes 688136 | tf_op jit(solution)/shard_map/ppermute | solution.py:15
  197.1 8.4 %collective-permute-done.3 = bf16[128,896]{1,0:T(8,128)(2,1)S(1)} collective-permute-done((bf16[128,896]{1,0:T(8,128)(2,1)S(1)}, bf16[128,896]{1,0:T(8,128)(2,1)S(1)}, u32[]{:S(2)}, u32[]{:S(2)}) %collective-permute-start.3) | collective-permute-done | bytes 229408 | tf_op jit(solution)/shard_map/ppermute | solution.py:15
  207.0 3.6 %collective-permute-start.4 = (bf16[128,896]{1,0:T(8,128)(2,1)}, bf16[128,896]{1,0:T(8,128)(2,1)}, u32[]{:S(2)}, u32[]{:S(2)}) collective-permute-start(bf16[128,896]{1,0:T(8,128)(2,1)} %fusion.18), channel_id=1, source_target_pairs={{0,16},{1,17},{2,18},{3,19},{4,20},{5,21},{6,22},{7,23},{8,24},{9,... | collective-permute-start | bytes 688136 | tf_op jit(solution)/shard_map/ppermute | solution.py:15
  210.5 28.3 %all-gather.2.cloned.1.call-done = bf16[2048,896]{1,0:T(8,128)(2,1)} async-done(((bf16[128,896]{1,0:T(8,128)(2,1)}), bf16[2048,896]{1,0:T(8,128)(2,1)}) %all-gather.2.cloned.1.call-update) | async-done | bytes 3670032 | tf_op jit(solution)/shard_map/all_gather | solution.py:79
  238.9 5.1 %multiply_convert_fusion.1 = bf16[896,512]{1,0:T(8,128)(2,1)} fusion(bf16[2048,896]{1,0:T(8,128)(2,1)} %all-gather.2.cloned.1.call-done, bf16[2048,512]{1,0:T(8,128)(2,1)S(1)} %bitcast.17), kind=kOutput, calls=%fused_computation.2 | convolution fusion | flops 1879965696 | bytes 6684672 | tf_op jit(solution)/shard_map/dot_general | solution.py:81
  244.0 1.8 fusion.6
  (33 shorter events, 4.8 us)
Async XLA Ops:
  7.2 67.3 %copy-start = (bf16[896,512]{1,0:T(8,128)(2,1)S(1)}, bf16[896,512]{1,0:T(8,128)(2,1)}, u32[]{:S(2)}) copy-start(bf16[896,512]{1,0:T(8,128)(2,1)} %param.8) | copy-start | bytes 2752516
  7.2 153.5 %reduce-scatter.2.cloned.1.call-start = ((), (), s32[]{:S(2)}) async-start(), calls=%async_computation.2 | async-start | bytes 3899392 | tf_op jit(solution)/shard_map/reduce_scatter | solution.py:67
  80.3 0.7 copy-start.7
  80.4 158.5 %all-gather.2.cloned.1.call-start = ((), (), s32[]{:S(2)}) async-start(), calls=%async_computation.3 | async-start | bytes 3899392 | tf_op jit(solution)/shard_map/all_gather | solution.py:79
  85.8 13.6 %copy-start.6 = (bf16[128,896]{1,0:T(8,128)(2,1)S(1)}, bf16[128,896]{1,0:T(8,128)(2,1)}, u32[]{:S(2)}) copy-start(bf16[128,896]{1,0:T(8,128)(2,1)} %param.6) | copy-start | bytes 688132
  99.9 3.4 %collective-permute-start.5 = (bf16[128,896]{1,0:T(8,128)(2,1)S(1)}, bf16[128,896]{1,0:T(8,128)(2,1)S(1)}, u32[]{:S(2)}, u32[]{:S(2)}) collective-permute-start(bf16[128,896]{1,0:T(8,128)(2,1)S(1)} %get-tuple-element.10), channel_id=1, source_target_pairs={{0,1},{1,0},{2,3},{3,2},{4,5},{5,4},{6,7},{7,6},{8,9},{9,8},{10,11... | collective-permute-start | bytes 688136 | tf_op jit(solution)/shard_map/ppermute | solution.py:15
  103.3 16.0 %copy-start.2 = (bf16[128,896]{1,0:T(8,128)(2,1)}, bf16[128,896]{1,0:T(8,128)(2,1)S(1)}, u32[]{:S(2)}) copy-start(bf16[128,896]{1,0:T(8,128)(2,1)S(1)} %collective-permute-done.5) | copy-start | bytes 688132
  104.0 43.5 %copy-start.8 = (s32[128]{0:T(128)S(1)}, s32[128]{0:T(128)}, u32[]{:S(2)}) copy-start(s32[128]{0:T(128)} %param.10) | copy-start | bytes 1540
  104.0 9.9 %collective-permute-start.6 = (bf16[128,896]{1,0:T(8,128)(2,1)}, bf16[128,896]{1,0:T(8,128)(2,1)S(1)}, u32[]{:S(2)}, u32[]{:S(2)}) collective-permute-start(bf16[128,896]{1,0:T(8,128)(2,1)} %fusion.21), channel_id=1, source_target_pairs={{0,2},{1,3},{2,0},{3,1},{4,6},{5,7},{6,4},{7,5},{8,10},{9,11},{10,... | collective-permute-start | bytes 688136 | tf_op jit(solution)/shard_map/ppermute | solution.py:15
  113.9 5.3 %copy-start.5 = (bf16[128,896]{1,0:T(8,128)(2,1)}, bf16[128,896]{1,0:T(8,128)(2,1)S(1)}, u32[]{:S(2)}) copy-start(bf16[128,896]{1,0:T(8,128)(2,1)S(1)} %collective-permute-done.6) | copy-start | bytes 688132
  114.7 13.9 %collective-permute-start.7 = (bf16[128,896]{1,0:T(8,128)(2,1)}, bf16[128,896]{1,0:T(8,128)(2,1)}, u32[]{:S(2)}, u32[]{:S(2)}) collective-permute-start(bf16[128,896]{1,0:T(8,128)(2,1)} %fusion.17), channel_id=1, source_target_pairs={{0,4},{1,5},{2,6},{3,7},{4,0},{5,1},{6,2},{7,3},{8,12},{9,13},{10,... | collective-permute-start | bytes 688136 | tf_op jit(solution)/shard_map/ppermute | solution.py:15
  130.7 13.9 %collective-permute-start.8 = (bf16[128,896]{1,0:T(8,128)(2,1)}, bf16[128,896]{1,0:T(8,128)(2,1)S(1)}, u32[]{:S(2)}, u32[]{:S(2)}) collective-permute-start(bf16[128,896]{1,0:T(8,128)(2,1)} %get-tuple-element.2), channel_id=1, source_target_pairs={{0,8},{1,9},{2,10},{3,11},{4,12},{5,13},{6,14},{7,15},{8,0},{9,1},... | collective-permute-start | bytes 688136 | tf_op jit(solution)/shard_map/ppermute | solution.py:15
  144.7 11.7 %collective-permute-start.9 = (bf16[128,896]{1,0:T(8,128)(2,1)S(1)}, bf16[128,896]{1,0:T(8,128)(2,1)}, u32[]{:S(2)}, u32[]{:S(2)}) collective-permute-start(bf16[128,896]{1,0:T(8,128)(2,1)S(1)} %fusion.16), channel_id=1, source_target_pairs={{0,16},{1,17},{2,18},{3,19},{4,20},{5,21},{6,22},{7,23},{8,24},{9,... | collective-permute-start | bytes 688136 | tf_op jit(solution)/shard_map/ppermute | solution.py:15
  162.5 3.4 %collective-permute-start = (bf16[128,896]{1,0:T(8,128)(2,1)S(1)}, bf16[128,896]{1,0:T(8,128)(2,1)S(1)}, u32[]{:S(2)}, u32[]{:S(2)}) collective-permute-start(bf16[128,896]{1,0:T(8,128)(2,1)S(1)} %get-tuple-element.8), channel_id=1, source_target_pairs={{0,1},{1,0},{2,3},{3,2},{4,5},{5,4},{6,7},{7,6},{8,9},{9,8},{10,11... | collective-permute-start | bytes 688136 | tf_op jit(solution)/shard_map/ppermute | solution.py:15
  165.9 73.0 %copy-start.1 = (bf16[16,128,512]{2,1,0:T(8,128)(2,1)S(1)}, bf16[16,128,512]{2,1,0:T(8,128)(2,1)}, u32[]{:S(2)}) copy-start(bf16[16,128,512]{2,1,0:T(8,128)(2,1)} %copy.11) | copy-start | bytes 6291460
  165.9 10.2 %collective-permute-start.1 = (bf16[128,896]{1,0:T(8,128)(2,1)S(1)}, bf16[128,896]{1,0:T(8,128)(2,1)S(1)}, u32[]{:S(2)}, u32[]{:S(2)}) collective-permute-start(bf16[128,896]{1,0:T(8,128)(2,1)S(1)} %fusion.22), channel_id=1, source_target_pairs={{0,2},{1,3},{2,0},{3,1},{4,6},{5,7},{6,4},{7,5},{8,10},{9,11},{10,... | collective-permute-start | bytes 688136 | tf_op jit(solution)/shard_map/ppermute | solution.py:15
  176.3 15.6 %collective-permute-start.2 = (bf16[128,896]{1,0:T(8,128)(2,1)S(1)}, bf16[128,896]{1,0:T(8,128)(2,1)S(1)}, u32[]{:S(2)}, u32[]{:S(2)}) collective-permute-start(bf16[128,896]{1,0:T(8,128)(2,1)S(1)} %fusion.19), channel_id=1, source_target_pairs={{0,4},{1,5},{2,6},{3,7},{4,0},{5,1},{6,2},{7,3},{8,12},{9,13},{10,... | collective-permute-start | bytes 688136 | tf_op jit(solution)/shard_map/ppermute | solution.py:15
  192.1 13.4 %collective-permute-start.3 = (bf16[128,896]{1,0:T(8,128)(2,1)S(1)}, bf16[128,896]{1,0:T(8,128)(2,1)S(1)}, u32[]{:S(2)}, u32[]{:S(2)}) collective-permute-start(bf16[128,896]{1,0:T(8,128)(2,1)S(1)} %get-tuple-element.4), channel_id=1, source_target_pairs={{0,8},{1,9},{2,10},{3,11},{4,12},{5,13},{6,14},{7,15},{8,0},{9,1},... | collective-permute-start | bytes 688136 | tf_op jit(solution)/shard_map/ppermute | solution.py:15
  205.5 0.7 copy-start.3
  207.0 37.0 %collective-permute-start.4 = (bf16[128,896]{1,0:T(8,128)(2,1)}, bf16[128,896]{1,0:T(8,128)(2,1)}, u32[]{:S(2)}, u32[]{:S(2)}) collective-permute-start(bf16[128,896]{1,0:T(8,128)(2,1)} %fusion.18), channel_id=1, source_target_pairs={{0,16},{1,17},{2,18},{3,19},{4,20},{5,21},{6,22},{7,23},{8,24},{9,... | collective-permute-start | bytes 688136 | tf_op jit(solution)/shard_map/ppermute | solution.py:15
  238.9 5.1 %copy-start.4 = (bf16[128,896]{1,0:T(8,128)(2,1)S(1)}, bf16[128,896]{1,0:T(8,128)(2,1)}, u32[]{:S(2)}) copy-start(bf16[128,896]{1,0:T(8,128)(2,1)} %copy-done.3) | copy-start | bytes 688132
Sparse Core Ops, SparseCore 0:
  80.5 80.1 reduce-scatter.1
  163.4 75.4 all-gather.1
where the time goes:
time: 254 us; the launch traced here: 253 us
  waiting for transfers between devices  91.8 us (36%)
  blocking collectives  60.5 us (24%)
  starting transfers between devices  38 us (15%)
  local copies, waits for them, and re-layouts  21.7 us (9%)
  between operations  14.2 us (6%)
  matrix products  13.2 us (5%)
  other arithmetic  13.2 us (5%)
    ppermute x10, waiting for transfers between devices, swapped(): return lax.ppermute(value, axis, pairs)  61 us
    all_to_all x1, blocking collectives, body(): lax.all_to_all(cotangent, 'dp', split_axis=1, concat_axis=0, tiled=True)  60.5 us
    ppermute x10, starting transfers between devices, swapped(): return lax.ppermute(value, axis, pairs)  37.9 us
    all_gather x1, waiting for transfers between devices, body(): shard_rows = lax.all_gather(quantized, 'dp', axis=0, tiled=True)  28.3 us
    convert_element_type x1, local copies, waits for them, and re-layouts, body(): jnp.kron(sylvester(group_rows), jnp.asarray(paley_table(), jnp.float32))  13.6 us
    dot_general x1, matrix products, body(): lax.dot_general(swapped_grad, weight, (((1,), (1,)), ((), ())), preferred...  5.9 us
    unnamed x19, local copies, waits for them, and re-layouts  5.47 us
    dot_general x1, matrix products, body(): lax.dot_general(shard_rows, grad_rows, (((0,), (0,)), ((), ())), preferre...  5.09 us
  transfers between devices with their start and end apart: 12, of which 11 were waited for; matrix products, arithmetic and copies ran while one was open for 13% of the time, Pallas kernels for 0%

commit v1 on v0

v1 whole, which is shorter than its diff:
```python
import itertools
import math

import jax
import jax.numpy as jnp
import numpy as np
from jax import lax
from jax.experimental import pallas as pl
from jax.experimental.pallas import tpu as pltpu
from jax.sharding import PartitionSpec as P

FF = 28672
MESH = pl.DeviceIdType.MESH
BF = jnp.bfloat16
F32 = jnp.float32
TR = 16


def paley_table():
    residues = set((number * number % 13 for number in range(1, 13)))
    jacobi = np.zeros((13, 13))
    for row_at in range(13):
        for col_at in range(13):
            differ = (col_at - row_at) % 13
            if differ != 0:
                jacobi[row_at, col_at] = 1.0 if differ in residues else -1.0
    confer = np.zeros((14, 14))
    confer[0, 1:] = 1.0
    confer[1:, 0] = 1.0
    confer[1:, 1:] = jacobi
    return np.kron(confer, np.array([[1.0, 1.0], [1.0, -1.0]])) + np.kron(
        np.eye(14), np.array([[1.0, -1.0], [-1.0, -1.0]])
    )


def sylvester(points):
    counter = np.arange(points)
    common = counter[:, None] & counter[None, :]
    parity = np.zeros((points, points), np.int64)
    for bit_pos in range(points.bit_length()):
        parity = parity + (common >> bit_pos & 1)
    return 1.0 - 2.0 * (parity % 2)


class Chunk:
    pass


def chunk_scratch(Z, Y, R, DB, w):
    K = Z // 2
    slices = (Y, TR, w)
    return dict(
        f_own=((R, w), F32), f_s0=((R, w), BF), f_r0=((R, w), BF), f_s1=((R, w), BF), f_r1=((R, w), BF),
        f_as=(slices, BF), f_ar=(slices, BF), f_b=(slices, BF), q=((Z,) + slices, BF),
        xs=((w, DB), BF), xr=((w, DB), BF), wown=((w, DB), F32),
        g=((Z, R, w), F32), rs_s=((2, K, R, w), BF), rs_r=((2, K, R, w), BF),
        b_own=((R, w), F32), b_s0=((R, w), BF), b_r0=((R, w), BF), b_s1=((R, w), BF), b_r1=((R, w), BF),
        b_as=(slices, BF), b_ar=(slices, BF), b_b=(slices, BF), b_q=(slices, BF),
    )


def kernel(cfg, act_h, cot_h, w_h, mask_h, scale_v, table_h, gin_o, wg_o, *scr):
    Z, Y, R, F, DB, chunks, norm, wscale, order = cfg
    K, KY = Z // 2, Y // 2
    NC = len(chunks)
    scr = list(scr)
    act_v, table_v, mask_v, wbuf, cbuf, step_v, lsem, ssem, rsem = scr[:9]
    del scr[:9]
    ch = []
    at = 0
    for w in chunks:
        one = Chunk()
        one.lo, one.w = at, w
        at += w
        for name in chunk_scratch(Z, Y, R, DB, w):
            setattr(one, name, scr.pop(0))
        ch.append(one)

    dp, tn = lax.axis_index("dp"), lax.axis_index("tensor")
    xl, z = lax.div(dp, Z), lax.rem(dp, Z)
    xh, y, c = lax.div(tn, 2 * Y), lax.rem(lax.div(tn, 2), Y), lax.rem(tn, 2)

    def dev(xl_=xl, z_=z, xh_=xh, y_=y, c_=c):
        return {"dp": xl_ * Z + z_, "tensor": (xh_ * Y + y_) * 2 + c_}

    def zz(k):
        return lax.rem(z + (k + Z), Z)

    def yy(k):
        return lax.rem(y + (k + Y), Y)

    count, lcount = itertools.count(), itertools.count()
    sent = []

    def send(src, dst, to):
        k = next(count)
        copy = pltpu.make_async_remote_copy(
            src_ref=src, dst_ref=dst, send_sem=ssem.at[k], recv_sem=rsem.at[k], device_id=to, device_id_type=MESH
        )
        copy.start()
        sent.append(copy)
        return copy

    def local(src, dst):
        copy = pltpu.make_async_copy(src, dst, lsem.at[next(lcount)])
        copy.start()
        return copy

    def arrived(copies):
        for copy in copies:
            copy.wait_recv()

    sc, sh = (1 - 2 * c).astype(F32), (1 - 2 * xh).astype(F32)
    y_rows = pl.multiple_of(y * TR, TR)

    act_c = local(act_h, act_v)
    table_c = local(table_h, table_v)
    cot_c = local(
        cot_h.at[pl.ds(y_rows, TR), pl.ds(pl.multiple_of((c * Z + z) * DB, DB), DB)], cbuf.at[c, z, y]
    )
    mask_c = local(mask_h, mask_v)
    w_c = local(w_h, wbuf.at[xl])
    barrier = pltpu.get_barrier_semaphore()
    peers = [dev(c_=1 - c), dev(xh_=1 - xh), dev(xl_=1 - xl)]
    peers += [dev(y_=yy(k)) for k in range(1, Y)] + [dev(z_=zz(k)) for k in range(1, Z)]
    for peer in peers:
        pl.semaphore_signal(barrier, inc=1, device_id=peer, device_id_type=MESH)
    exponent = jnp.broadcast_to(scale_v[...], (R, R)).T
    step_v[...] = jnp.left_shift(jnp.ones_like(exponent), exponent + 3).astype(F32) * 0.125
    pl.semaphore_wait(barrier, len(peers))

    st = {}

    def cot_z():
        st["cz"] = [
            send(
                cot_h.at[pl.ds(y_rows, TR), pl.ds(pl.multiple_of((c * Z + zz(k)) * DB, DB), DB)],
                cbuf.at[c, z, y],
                dev(z_=zz(k)),
            )
            for k in range(1, Z)
        ]

    st["cc"] = []

    def core_share(view):
        st["cc"].append(send(view, view, dev(c_=1 - c)))

    def cot_y(s):
        if s == 0:
            cot_c.wait()
            arrived(st["cz"])
        else:
            arrived(st["cy"])
        if s < KY:
            last = s == KY - 1
            zr, zl = (pl.ds(0, Z // 2), pl.ds(Z // 2, Z // 2)) if last else (pl.ds(0, Z),) * 2
            right, left = cbuf.at[c, zr, yy(-s)], cbuf.at[c, zl, yy(s)]
            st["cy"] = [send(right, right, dev(y_=yy(1))), send(left, left, dev(y_=yy(-1)))]
        if s == 0:
            core_share(cbuf.at[c, :, y])
        elif s < KY:
            core_share(cbuf.at[c, :, yy(-s)])
            core_share(cbuf.at[c, :, yy(s)])
        else:
            core_share(cbuf.at[c, :, yy(s)])

    def cot_end():
        arrived(st["cc"])

    def weights(j):
        k = ch[j]
        rows = pl.ds(k.lo, k.w)
        k.wc = send(w_h.at[rows], wbuf.at[xl, rows], dev(xl_=1 - xl))

    def to_core(k, p, value):
        own, s0, r0 = getattr(k, p + "own"), getattr(k, p + "s0"), getattr(k, p + "r0")
        own[...] = value
        s0[...] = value.astype(BF)
        st[p, k, "c"] = [send(s0, r0, dev(c_=1 - c))]

    def to_xh(k, p):
        own, r0, s1, r1 = (getattr(k, p + n) for n in ("own", "r0", "s1", "r1"))
        arrived(st[p, k, "c"])
        value = r0[...].astype(F32) + sc * own[...]
        own[...] = value
        s1[...] = value.astype(BF)
        st[p, k, "x"] = [send(s1, r1, dev(xh_=1 - xh))]

    def to_y(k, p):
        own, r1, a_s, a_r = (getattr(k, p + n) for n in ("own", "r1", "as", "ar"))
        arrived(st[p, k, "x"])
        value = r1[...].astype(F32) + sh * own[...]
        a_s[...] = value.astype(BF).reshape(a_s.shape)
        st[p, k, "a"] = [send(a_s.at[yy(n)], a_r.at[y], dev(y_=yy(n))) for n in range(1, Y)]
        a_r[pl.ds(y, 1)] = a_s[pl.ds(y, 1)]

    def hada_y(k, p):
        a_r = getattr(k, p + "ar")
        arrived(st[p, k, "a"])
        parts = [a_r[n].astype(F32) for n in range(Y)]
        apart = 1
        while apart < Y:
            parts = [
                parts[n] + parts[n ^ apart] if not n & apart else parts[n ^ apart] - parts[n] for n in range(Y)
            ]
            apart *= 2
        return parts

    def back_y(k, p, target):
        b = getattr(k, p + "b")
        st[p, k, "b"] = [send(b.at[yy(n)], target.at[y], dev(y_=yy(n))) for n in range(1, Y)]
        target[pl.ds(y, 1)] = b[pl.ds(y, 1)]

    def f0(j):
        k = ch[j]
        if j == 0:
            act_c.wait()
            table_c.wait()
        to_core(k, "f_", jnp.dot(act_v[...], table_v[:, pl.ds(k.lo, k.w)], preferred_element_type=F32))

    def f1(j):
        to_xh(ch[j], "f_")

    def f2(j):
        to_y(ch[j], "f_")

    def f3(j):
        k = ch[j]
        parts = hada_y(k, "f_")
        step = step_v[pl.ds(y_rows, TR), :][:, 0:1]
        for n in range(Y):
            k.f_b[n] = jnp.clip(parts[n] * norm, -8.0 * step, 7.0 * step).astype(BF)
        back_y(k, "f_", k.q.at[z])

    def ag(j, s):
        k = ch[j]
        arrived(st["f_", k, "b"] if s == 0 else k.agc)
        if s < K:
            last = s == K - 1
            yr, yl = (pl.ds(0, Y // 2), pl.ds(Y // 2, Y // 2)) if last else (pl.ds(0, Y),) * 2
            right, left = k.q.at[zz(-s), yr], k.q.at[zz(s), yl]
            k.agc = [send(right, right, dev(z_=zz(1))), send(left, left, dev(z_=zz(-1)))]

    def wg_dot(k, half, out, cast):
        block = 128

        def step(n, _):
            cols = pl.ds(pl.multiple_of(n * block, block), block)
            rows = k.q[:, :, :, cols].reshape(Z * R, block)
            cot = cbuf[pl.ds(half, 1)].reshape(Z * R, DB)
            out[cols, :] = lax.dot_general(
                rows, cot, (((0,), (0,)), ((), ())), preferred_element_type=F32
            ).astype(cast)
            return _

        lax.fori_loop(0, k.w // block, step, 0)

    def wg(j):
        k = ch[j]
        wg_dot(k, 1 - xl, k.xs, BF)
        k.xc = send(k.xs, k.xr, dev(xl_=1 - xl))
        wg_dot(k, xl, k.wown, F32)

    def wend(j):
        k = ch[j]
        k.xc.wait_recv()
        wg_o[pl.ds(k.lo, k.w), :] = ((k.wown[...] + k.xr[...].astype(F32)) * wscale).astype(BF)

    def grad(j):
        k = ch[j]
        if j == 0:
            w_c.wait()
        k.wc.wait_recv()
        rows = pl.ds(k.lo, k.w)
        block = 2 if Z % 2 == 0 else 1

        def step(n, _):
            zs = pl.ds(n * block, block)
            total = jnp.zeros((block * R, k.w), F32)
            for half in range(2):
                total = total + lax.dot_general(
                    cbuf[half, zs].reshape(block * R, DB),
                    wbuf[half, rows, :],
                    (((1,), (1,)), ((), ())),
                    preferred_element_type=F32,
                )
            k.g[zs] = total.reshape(block, R, k.w)
            return _

        lax.fori_loop(0, Z // block, step, 0)

    top, bottom = pl.ds(0, R // 2), pl.ds(R // 2, R // 2)

    def rs(j, s):
        k = ch[j]
        if s == 0:
            for way, rows, to in ((0, top, 1), (1, bottom, -1)):
                k.rs_s[way, 0, rows, :] = k.g[zz(K), rows, :].astype(BF)
            k.rsc = [
                send(k.rs_s.at[way, 0, rows], k.rs_r.at[way, 0, rows], dev(z_=zz(to)))
                for way, rows, to in ((0, top, 1), (1, bottom, -1))
            ]
            return
        before = k.rsc
        k.rsc = []
        for way, rows, to in ((0, top, 1), (1, bottom, -1)):
            before[way].wait_recv()
            dest = zz(to * (K - s))
            if s == 1:
                other = bottom if way == 0 else top
                k.rs_s[way, 1, rows, :] = (k.g[dest, rows, :] + k.rs_r[way, 0, rows, :].astype(F32)).astype(BF)
                k.rs_s[way, 1, other, :] = k.g[dest, other, :].astype(BF)
            else:
                k.rs_s[way, s] = (k.g[dest] + k.rs_r[way, s - 1].astype(F32)).astype(BF)
            k.rsc.append(send(k.rs_s.at[way, s], k.rs_r.at[way, s], dev(z_=zz(to))))

    def b0(j):
        k = ch[j]
        if j == 0:
            mask_c.wait()
        arrived(k.rsc)
        total = k.g[z] + k.rs_r[0, K - 1].astype(F32) + k.rs_r[1, K - 1].astype(F32)
        mask = mask_v[:, pl.ds(k.lo, k.w)].astype(F32)
        to_core(k, "b_", (mask * total).astype(BF).astype(F32))

    def b1(j):
        to_xh(ch[j], "b_")

    def b2(j):
        to_y(ch[j], "b_")

    def b3(j):
        k = ch[j]
        parts = hada_y(k, "b_")
        for n in range(Y):
            k.b_b[n] = parts[n].astype(BF)
        back_y(k, "b_", k.b_q)

    def bend():
        total = jnp.zeros((R, F), F32)
        for k in ch:
            arrived(st["b_", k, "b"])
            total = total + jnp.dot(
                k.b_q[...].reshape(R, k.w), table_v[pl.ds(k.lo, k.w), :], preferred_element_type=F32
            )
        gin_o[...] = (total * norm).astype(BF)

    tasks = dict(locals())
    for name, *args in order(NC, K, KY):
        tasks[name](*args)
    for copy in sent:
        copy.wait_send()


def copies_of(NC, Z, Y):
    cot = (Z - 1) + 2 * (Y // 2) + Y
    each = 1 + 2 * (2 + 2 * (Y - 1)) + 4 * (Z // 2) + 1
    return cot + NC * each


def plan(NC, K, KY):
    J = range(NC)
    todo = [("cot_z",)]
    todo += [("f0", j) for j in J]
    todo += [("f1", j) for j in J]
    todo += [("weights", j) for j in J]
    todo += [("cot_y", 0)]
    todo += [("f2", j) for j in J]
    todo += [("cot_y", 1)]
    todo += [("f3", j) for j in J]
    todo += [("cot_y", s) for s in range(2, KY)]
    todo += [("ag", j, 0) for j in J]
    todo += [("cot_y", KY), ("cot_end",)]
    for j in J:
        todo += [("grad", j), ("rs", j, 0)]
    for s in range(1, K):
        todo += [("ag", j, s) for j in J]
        todo += [("rs", j, s) for j in J]
    for j in J:
        todo += [("b0", j), ("ag", j, K), ("wg", j)]
    todo += [("b1", j) for j in J]
    todo += [("b2", j) for j in J]
    todo += [("b3", j) for j in J]
    todo += [("bend",)]
    todo += [("wend", j) for j in J]
    return todo


def call(Z, Y, R, F, DB, chunks, norm, wscale, order, args):
    scratch = [
        pltpu.VMEM((R, F), BF), pltpu.VMEM((F, F), BF), pltpu.VMEM((R, F), jnp.int32),
        pltpu.VMEM((2, F, DB), BF), pltpu.VMEM((2, Z, Y, TR, DB), BF), pltpu.VMEM((R, R), F32),
        pltpu.SemaphoreType.DMA((5,)),
    ]
    total = copies_of(len(chunks), Z, Y)
    scratch += [pltpu.SemaphoreType.DMA((total,)), pltpu.SemaphoreType.DMA((total,))]
    for w in chunks:
        scratch += [pltpu.VMEM(*spec) for spec in chunk_scratch(Z, Y, R, DB, w).values()]
    cfg = (Z, Y, R, F, DB, chunks, norm, wscale, order)
    hbm, vmem = pl.BlockSpec(memory_space=pl.ANY), pl.BlockSpec(memory_space=pltpu.VMEM)

    def run(*refs):
        kernel(cfg, *refs)

    return pl.pallas_call(
        run,
        out_shape=(jax.ShapeDtypeStruct((R, F), BF), jax.ShapeDtypeStruct((F, DB), BF)),
        in_specs=[hbm, hbm, hbm, hbm, vmem, hbm],
        out_specs=(vmem, vmem),
        scratch_shapes=scratch,
        compiler_params=pltpu.CompilerParams(
            collective_id=0, has_side_effects=True, vmem_limit_bytes=52 * 2**20
        ),
    )(*args)


def body(activations, cotangent, weight, clip_mask, scale_exponent):
    R, F = activations.shape
    DB = weight.shape[1]
    table = jnp.asarray(np.kron(sylvester(F // 28), paley_table()), BF)
    tokens = R * lax.axis_size("dp")
    return call(
        8, 8, R, F, DB, (512, 384), 1.0 / math.sqrt(FF), 1.0 / math.sqrt(tokens), plan,
        (activations, cotangent, weight, clip_mask, scale_exponent.reshape(1, R), table),
    )


def solution(mesh):
    return jax.shard_map(
        body,
        mesh=mesh,
        in_specs=(P("dp", "tensor"), P("dp", None), P("tensor", "dp"), P("dp", "tensor"), P("dp")),
        out_specs=(P("dp", "tensor"), P("tensor", "dp")),
        check_vma=False,
    )
```

time: 254 us -> 128 us (0.50)
  the two profiles are of different devices: /device:TPU:12 before, /device:TPU:1 now
where the time goes in v1:
time: 128 us
  Pallas kernels  123 us (96%)
  local copies, waits for them, and re-layouts  4.22 us (3%)
    pallas_call x1, Pallas kernels, call(): pl.pallas_call(run, out_shape=(jax.ShapeDtypeStruct((R, F), BF), jax.Shap...  123 us
    unnamed x8, local copies, waits for them, and re-layouts  4.22 us

profile of v1, /device:TPU:1, one launch (start us, length us, event | category | flops | bytes accessed | tf_op | source)
XLA Modules:
  0.0 127.7 jit_solution(17431792444260341023)
XLA Ops:
  0.6 0.0 copy-start
  0.6 1.0 copy-done
  1.7 0.0 copy-start.1
  1.7 0.9 copy-done.1
  2.6 0.0 copy-start.2
  2.6 0.7 copy-done.2
  3.2 122.8 %shard_map.77 = (bf16[128,896]{1,0:T(8,128)(2,1)S(1)}, bf16[896,512]{1,0:T(8,128)(2,1)S(1)}) custom-call(bf16[128,896]{1,0:T(8,128)(2,1)S(1)} %copy-done.1, bf16[128,8192]{1,0:T(8,128)(2,1)} %refs_1_.1, bf16[896,512]{1,0:T(8,128)(2,1)} %refs_2_.1, s32[128,896]{1,0:T(8,128)S(1)} %copy-done, s32[1,128]{1,0:T(1,128)S(1)} %bitcast.1, ...), custom_call_target="tpu_custom_call" | custom-call | tf_op jit(solution)/shard_map/pallas_call | solution.py:406
  126.1 0.7 copy.10
  126.8 0.9 copy.11
Async XLA Ops:
  0.6 1.0 copy-start
  1.7 0.9 copy-start.1
  2.6 0.7 copy-start.2

commit v2 on v1

v2 whole, which is shorter than its diff:
```python
import itertools
import math

import jax
import jax.numpy as jnp
import numpy as np
from jax import lax
from jax.experimental import pallas as pl
from jax.experimental.pallas import tpu as pltpu
from jax.sharding import PartitionSpec as P

FF = 28672
MESH = pl.DeviceIdType.MESH
BF = jnp.bfloat16
F32 = jnp.float32
TR = 16
PIECES = 4


def paley_table():
    residues = set((number * number % 13 for number in range(1, 13)))
    jacobi = np.zeros((13, 13))
    for row_at in range(13):
        for col_at in range(13):
            differ = (col_at - row_at) % 13
            if differ != 0:
                jacobi[row_at, col_at] = 1.0 if differ in residues else -1.0
    confer = np.zeros((14, 14))
    confer[0, 1:] = 1.0
    confer[1:, 0] = 1.0
    confer[1:, 1:] = jacobi
    return np.kron(confer, np.array([[1.0, 1.0], [1.0, -1.0]])) + np.kron(
        np.eye(14), np.array([[1.0, -1.0], [-1.0, -1.0]])
    )


def sylvester(points):
    counter = np.arange(points)
    common = counter[:, None] & counter[None, :]
    parity = np.zeros((points, points), np.int64)
    for bit_pos in range(points.bit_length()):
        parity = parity + (common >> bit_pos & 1)
    return 1.0 - 2.0 * (parity % 2)


class Chunk:
    pass


def padded(w):
    return -(-w // 256) * 256


def chunk_scratch(Z, Y, R, DB, w):
    K = Z // 2
    wide, half = (Y, TR, padded(w)), (2, Y, TR, padded(w) // 2)
    return dict(
        f_own=((R, w), F32), f_s0=((R, w), BF), f_r0=((R, w), BF),
        f_as=(wide, BF), f_ar=(half, BF), f_b=(half, BF), q=((Z,) + wide, BF),
        xs=((w, DB), BF), xr=((w, DB), BF), wown=((w, DB), F32),
        g=((Z, R, w), F32), rs_s=((2, K, R, w), BF), rs_r=((2, K, R, w), BF),
        b_own=((R, w), F32), b_s0=((R, w), BF), b_r0=((R, w), BF),
        b_as=(wide, BF), b_ar=(half, BF), b_b=(half, BF), b_q=(wide, BF),
    )


class Once:
    made = []

    def __init__(self, wait):
        self.run, self.done = wait, False
        Once.made.append(self)

    def wait(self):
        if not self.done:
            self.run()
        self.done = True


def kernel(cfg, act_h, cot_h, w_h, mask_h, scale_h, table_h, gin_o, wg_o, *scr):
    Z, Y, R, F, DB, chunks, norm, wscale, order = cfg
    K = Z // 2
    NC = len(chunks)
    scr = list(scr)
    act_v, table_v, mask_v, scale_v, wbuf, cbuf, step_v, gin_v, lsem, ssem, rsem = scr[:11]
    del scr[:11]
    ch = []
    at = 0
    for w in chunks:
        one = Chunk()
        one.lo, one.w, one.half = at, w, padded(w) // 2
        at += w
        for name in chunk_scratch(Z, Y, R, DB, w):
            setattr(one, name, scr.pop(0))
        ch.append(one)

    dp, tn = lax.axis_index("dp"), lax.axis_index("tensor")
    xl, z = lax.div(dp, Z), lax.rem(dp, Z)
    xh, y, c = lax.div(tn, 2 * Y), lax.rem(lax.div(tn, 2), Y), lax.rem(tn, 2)
    piece = lax.rem(y, PIECES)

    def dev(xl_=xl, z_=z, xh_=xh, y_=y, c_=c):
        return {"dp": xl_ * Z + z_, "tensor": (xh_ * Y + y_) * 2 + c_}

    def zz(k):
        return lax.rem(z + (k + Z), Z)

    def yy(k):
        return lax.rem(y + (k + Y), Y)

    count, lcount = itertools.count(), itertools.count()
    Once.made = []

    def send(src, dst, to):
        k = next(count)
        copy = pltpu.make_async_remote_copy(
            src_ref=src, dst_ref=dst, send_sem=ssem.at[k], recv_sem=rsem.at[k], device_id=to, device_id_type=MESH
        )
        copy.start()
        one = Once(copy.wait_recv)
        one.left = Once(copy.wait_send)
        return one

    def local(src, dst):
        copy = pltpu.make_async_copy(src, dst, lsem.at[next(lcount)])
        copy.start()
        return Once(copy.wait)

    def arrived(copies):
        for copy in copies:
            copy.wait()

    sc = (1 - 2 * c).astype(F32)
    y_rows = pl.multiple_of(y * TR, TR)
    far = sorted(range(Y), key=lambda n: -min(n, Y - n))
    others = [(h, n) for n in far for h in (1, 0) if (h, n) != (0, 0)]

    def mates(h):
        return 1 - xh if h else xh

    PR = R // PIECES
    mine = pl.multiple_of(piece * PR, PR)

    def cot_block(dest):
        return cot_h.at[pl.ds(mine, PR), pl.ds(pl.multiple_of((c * Z + dest) * DB, DB), DB)]

    scale_c = local(scale_h, scale_v)
    act_c = local(act_h, act_v)
    table_c = local(table_h, table_v)
    cot_c = local(cot_block(z), cbuf.at[c, z, pl.ds(mine, PR)])
    mask_c = local(mask_h, mask_v)
    w_c = local(w_h, wbuf.at[xl])
    barrier = pltpu.get_barrier_semaphore()
    peers = [dev(c_=1 - c), dev(xl_=1 - xl)]
    peers += [dev(xh_=mates(h), y_=yy(n)) for h, n in others] + [dev(z_=zz(k)) for k in range(1, Z)]
    for peer in peers:
        pl.semaphore_signal(barrier, inc=1, device_id=peer, device_id_type=MESH)
    for k in ch:
        if 2 * k.half > k.w:
            blank = jnp.zeros((Y, TR, 2 * k.half - k.w), BF)
            k.f_as[:, :, pl.ds(k.w, 2 * k.half - k.w)] = blank
            k.b_as[:, :, pl.ds(k.w, 2 * k.half - k.w)] = blank
    scale_c.wait()
    exponent = jnp.broadcast_to(scale_v[...], (R, R)).T
    step_v[...] = jnp.left_shift(jnp.ones_like(exponent), exponent + 3).astype(F32) * 0.125
    act_c.wait()
    table_c.wait()
    for k in ch:
        value = jnp.dot(act_v[...], table_v[:, pl.ds(k.lo, k.w)], preferred_element_type=F32)
        k.f_own[...] = value
        k.f_s0[...] = value.astype(BF)
    pl.semaphore_wait(barrier, len(peers))

    st = {}

    def cot_z():
        st["cz"] = {0: cot_c}
        for k in sorted(range(1, Z), key=lambda k: -min(k, Z - k)):
            st["cz"][k] = send(cot_block(zz(k)), cbuf.at[c, z, pl.ds(mine, PR)], dev(z_=zz(k)))

    st["cy"], st["cc"] = {}, {}

    def cot_fwd(k):
        st["cz"][k].wait()
        source = zz(-k)
        whole = cbuf.at[c, source, pl.ds(mine, PR)]
        first = cbuf.at[c, source, pl.ds(mine, PR // 2)]
        second = cbuf.at[c, source, pl.ds(pl.multiple_of(mine + PR // 2, PR // 2), PR // 2)]
        st["cy"][k] = [
            send(view, view, dev(y_=yy(n))) for view, n in ((first, 2), (second, -2), (whole, 1), (whole, -1))
        ]

    def cot_in(k):
        arrived(st["cy"][k])
        block = cbuf.at[c, zz(-k)]
        st["cc"][k] = send(block, block, dev(c_=1 - c))

    def weights(j):
        k = ch[j]
        rows = pl.ds(k.lo, k.w)
        if j > 0:
            ch[j - 1].wc.left.wait()
        k.wc = send(w_h.at[rows], wbuf.at[xl, rows], dev(xl_=1 - xl))

    def to_core(k, p):
        st[p, k, "c"] = [send(getattr(k, p + "s0"), getattr(k, p + "r0"), dev(c_=1 - c))]

    def lanes(k, h):
        return pl.ds(pl.multiple_of(mates(h) * k.half, 128), k.half)

    def to_y(k, p):
        own, r0, a_s, a_r = (getattr(k, p + n) for n in ("own", "r0", "as", "ar"))
        arrived(st[p, k, "c"])
        value = r0[...].astype(F32) + sc * own[...]
        a_s[:, :, pl.ds(0, k.w)] = value.astype(BF).reshape(Y, TR, k.w)
        st[p, k, "a"] = [
            send(a_s.at[yy(n), :, lanes(k, h)], a_r.at[xh, y], dev(xh_=mates(h), y_=yy(n))) for h, n in others
        ]
        own_rows = a_s[pl.ds(y, 1)]
        a_r[pl.ds(xh, 1), pl.ds(y, 1)] = jnp.where(xh == 0, own_rows[:, :, : k.half], own_rows[:, :, k.half :])[None]

    def hada(k, p):
        a_r = getattr(k, p + "ar")
        arrived(st[p, k, "a"])
        parts = [a_r[n // Y, n % Y].astype(F32) for n in range(2 * Y)]
        apart = 1
        while apart < 2 * Y:
            parts = [
                parts[n] + parts[n ^ apart] if not n & apart else parts[n ^ apart] - parts[n] for n in range(2 * Y)
            ]
            apart *= 2
        return parts

    def back_y(k, p, target):
        b = getattr(k, p + "b")
        st[p, k, "b"] = [
            send(b.at[mates(h), yy(n)], target.at[y, :, lanes(k, 0)], dev(xh_=mates(h), y_=yy(n))) for h, n in others
        ]
        for h in range(2):

            @pl.when(xh == h)
            def _():
                target[pl.ds(y, 1), :, pl.ds(h * k.half, k.half)] = b[h, pl.ds(y, 1)]

    def f0(j):
        to_core(ch[j], "f_")

    def f1(j):
        to_y(ch[j], "f_")

    def f2(j):
        k = ch[j]
        parts = hada(k, "f_")
        step = step_v[pl.ds(y_rows, TR), :][:, 0:1]
        for n in range(2 * Y):
            k.f_b[n // Y, n % Y] = jnp.clip(parts[n] * norm, -8.0 * step, 7.0 * step).astype(BF)
        back_y(k, "f_", k.q.at[z])

    def ag(j, s):
        k = ch[j]
        arrived(st["f_", k, "b"] if s == 0 else k.agc)
        if s < K:
            last = s == K - 1
            yr, yl = (pl.ds(0, Y // 2), pl.ds(Y // 2, Y // 2)) if last else (pl.ds(0, Y),) * 2
            cols = pl.ds(0, k.w)
            right, left = k.q.at[zz(-s), yr, :, cols], k.q.at[zz(s), yl, :, cols]
            k.agc = [send(right, right, dev(z_=zz(1))), send(left, left, dev(z_=zz(-1)))]

    def wg_dot(k, half, cast):
        rows = k.q[:, :, :, pl.ds(0, k.w)].reshape(Z * R, k.w)
        cot = cbuf[pl.ds(half, 1)].reshape(Z * R, DB)
        return lax.dot_general(rows, cot, (((0,), (0,)), ((), ())), preferred_element_type=F32).astype(cast)

    def wg(j):
        k = ch[j]
        arrived(st["cc"].values())
        k.xs[...] = wg_dot(k, 1 - xl, BF)
        k.xc = send(k.xs, k.xr, dev(xl_=1 - xl))
        k.wown[...] = wg_dot(k, xl, F32)

    def wend(j):
        k = ch[j]
        k.xc.wait()
        wg_o[pl.ds(k.lo, k.w), :] = ((k.wown[...] + k.xr[...].astype(F32)) * wscale).astype(BF)

    def grad(j, s):
        k = ch[j]
        w_c.wait()
        k.wc.wait()
        for near in {(K - s) % Z, (s - K) % Z}:
            st["cc"][near].wait()
        rows = pl.ds(k.lo, k.w)
        dests = [zz(K - s)] if s in (0, K) else [zz(K - s), zz(s - K)]
        total = None
        for half in range(2):
            cot = jnp.concatenate([cbuf[half, pl.ds(dest, 1)].reshape(R, DB) for dest in dests], 0)
            part = lax.dot_general(cot, wbuf[half, rows, :], (((1,), (1,)), ((), ())), preferred_element_type=F32)
            total = part if total is None else total + part
        for n, dest in enumerate(dests):
            k.g[pl.ds(dest, 1)] = total[n * R : (n + 1) * R][None]

    top, bottom = pl.ds(0, R // 2), pl.ds(R // 2, R // 2)

    def rs(j, s):
        k = ch[j]
        if s == 0:
            for way, rows, to in ((0, top, 1), (1, bottom, -1)):
                k.rs_s[way, 0, rows, :] = k.g[zz(K), rows, :].astype(BF)
            k.rsc = [
                send(k.rs_s.at[way, 0, rows], k.rs_r.at[way, 0, rows], dev(z_=zz(to)))
                for way, rows, to in ((0, top, 1), (1, bottom, -1))
            ]
            return
        before = k.rsc
        k.rsc = []
        for way, rows, to in ((0, top, 1), (1, bottom, -1)):
            before[way].wait()
            dest = zz(to * (K - s))
            if s == 1:
                other = bottom if way == 0 else top
                k.rs_s[way, 1, rows, :] = (k.g[dest, rows, :] + k.rs_r[way, 0, rows, :].astype(F32)).astype(BF)
                k.rs_s[way, 1, other, :] = k.g[dest, other, :].astype(BF)
            else:
                k.rs_s[way, s] = (k.g[dest] + k.rs_r[way, s - 1].astype(F32)).astype(BF)
            k.rsc.append(send(k.rs_s.at[way, s], k.rs_r.at[way, s], dev(z_=zz(to))))

    def b0(j):
        k = ch[j]
        mask_c.wait()
        arrived(k.rsc)
        total = k.g[z] + k.rs_r[0, K - 1].astype(F32) + k.rs_r[1, K - 1].astype(F32)
        mask = mask_v[:, pl.ds(k.lo, k.w)].astype(F32)
        masked = (mask * total).astype(BF)
        k.b_own[...] = masked.astype(F32)
        k.b_s0[...] = masked
        to_core(k, "b_")

    def b1(j):
        to_y(ch[j], "b_")

    def b2(j):
        k = ch[j]
        parts = hada(k, "b_")
        for n in range(2 * Y):
            k.b_b[n // Y, n % Y] = parts[n].astype(BF)
        back_y(k, "b_", k.b_q)

    def b3(j):
        k = ch[j]
        arrived(st["b_", k, "b"])
        part = jnp.dot(
            k.b_q[:, :, pl.ds(0, k.w)].reshape(R, k.w), table_v[pl.ds(k.lo, k.w), :], preferred_element_type=F32
        )
        if j > 0:
            part = part + gin_v[...]
        if j < NC - 1:
            gin_v[...] = part
        else:
            gin_o[...] = (part * norm).astype(BF)

    tasks = dict(locals())
    for name, *args in order(NC, Z):
        tasks[name](*args)
    for one in Once.made:
        one.wait()


def copies_of(NC, Z, Y):
    cot = (Z - 1) + 5 * Z
    each = 1 + 2 * (1 + 2 * (2 * Y - 1)) + 4 * (Z // 2) + 1
    return cot + NC * each


STEPS = (
    ('f0', 1), ('cot_z',), ('f0', 0), ('f1', 1), ('f1', 0), ('cot_fwd', 7), ('weights', 0), ('f0', 2), ('f1', 2),
    ('cot_fwd', 2), ('cot_fwd', 1), ('f2', 0), ('f2', 1), ('f2', 2), ('weights', 1), ('cot_fwd', 6),
    ('cot_fwd', 5), ('ag', 0, 0), ('cot_in', 2), ('cot_in', 1), ('cot_fwd', 4), ('ag', 1, 0), ('cot_in', 5),
    ('cot_fwd', 3), ('ag', 0, 1), ('cot_in', 4), ('ag', 2, 0), ('cot_in', 6), ('weights', 2), ('ag', 1, 1),
    ('cot_in', 3), ('grad', 0, 0), ('cot_in', 7), ('rs', 0, 0), ('grad', 1, 0), ('rs', 1, 0), ('cot_fwd', 0),
    ('ag', 2, 1), ('grad', 1, 1), ('grad', 0, 1), ('ag', 1, 2), ('rs', 0, 1), ('grad', 0, 2), ('grad', 1, 3),
    ('grad', 0, 3), ('grad', 1, 2), ('grad', 2, 0), ('rs', 2, 0), ('rs', 1, 1), ('grad', 2, 3), ('cot_in', 0),
    ('ag', 1, 3), ('rs', 0, 2), ('grad', 2, 1), ('grad', 2, 2), ('grad', 0, 4), ('rs', 2, 1), ('grad', 2, 4),
    ('ag', 2, 2), ('ag', 1, 4), ('rs', 1, 2), ('wg', 1), ('rs', 0, 3), ('rs', 2, 2), ('rs', 1, 3), ('grad', 1, 4),
    ('rs', 2, 3), ('ag', 2, 3), ('b0', 0), ('b1', 0), ('b0', 1), ('b1', 1), ('b0', 2), ('ag', 0, 2), ('ag', 2, 4),
    ('wg', 2), ('b1', 2), ('b2', 0), ('ag', 0, 3), ('b2', 1), ('b2', 2), ('ag', 0, 4), ('wg', 0), ('b3', 0),
    ('wend', 1), ('b3', 1), ('b3', 2), ('wend', 2), ('wend', 0),
)


def plan(NC, Z):
    return STEPS


def call(Z, Y, R, F, DB, chunks, norm, wscale, order, args):
    scratch = [
        pltpu.VMEM((R, F), BF), pltpu.VMEM((F, F), BF), pltpu.VMEM((R, F), jnp.int32), pltpu.VMEM((1, R), jnp.int32),
        pltpu.VMEM((2, F, DB), BF), pltpu.VMEM((2, Z, R, DB), BF), pltpu.VMEM((R, R), F32), pltpu.VMEM((R, F), F32),
        pltpu.SemaphoreType.DMA((6,)),
    ]
    total = copies_of(len(chunks), Z, Y)
    scratch += [pltpu.SemaphoreType.DMA((total,)), pltpu.SemaphoreType.DMA((total,))]
    for w in chunks:
        scratch += [pltpu.VMEM(*spec) for spec in chunk_scratch(Z, Y, R, DB, w).values()]
    cfg = (Z, Y, R, F, DB, chunks, norm, wscale, order)
    hbm, vmem = pl.BlockSpec(memory_space=pltpu.HBM), pl.BlockSpec(memory_space=pltpu.VMEM)

    def run(*refs):
        kernel(cfg, *refs)

    return pl.pallas_call(
        run,
        out_shape=(jax.ShapeDtypeStruct((R, F), BF), jax.ShapeDtypeStruct((F, DB), BF)),
        in_specs=[hbm] * 6,
        out_specs=(vmem, vmem),
        scratch_shapes=scratch,
        compiler_params=pltpu.CompilerParams(
            collective_id=0, has_side_effects=True, vmem_limit_bytes=52 * 2**20
        ),
    )(*args)


def body(activations, cotangent, weight, clip_mask, scale_exponent):
    R, F = activations.shape
    DB = weight.shape[1]
    table = jnp.asarray(np.kron(sylvester(F // 28), paley_table()), BF)
    tokens = R * lax.axis_size("dp")
    return call(
        8, 8, R, F, DB, (256, 384, 256), 1.0 / math.sqrt(FF), 1.0 / math.sqrt(tokens), plan,
        (activations, cotangent, weight, clip_mask, scale_exponent.reshape(1, R), table),
    )


def solution(mesh):
    return jax.shard_map(
        body,
        mesh=mesh,
        in_specs=(P("dp", "tensor"), P("dp", None), P("tensor", "dp"), P("dp", "tensor"), P("dp")),
        out_specs=(P("dp", "tensor"), P("tensor", "dp")),
        check_vma=False,
    )
```

time: 128 us -> 100 us (0.78)
  Pallas kernels: 123 us -> 95.2 us
    pallas_call x1, Pallas kernels: 123 us -> 95.2 us  [call(): pl.pallas_call(run, out_shape=(jax.ShapeDtypeStruct((R, F), BF), jax.Shap...]
where the time goes in v2:
time: 100 us
  Pallas kernels  95.2 us (95%)
  local copies, waits for them, and re-layouts  4.22 us (4%)
    pallas_call x1, Pallas kernels, call(): pl.pallas_call(run, out_shape=(jax.ShapeDtypeStruct((R, F), BF), jax.Shap...  95.2 us
    unnamed x8, local copies, waits for them, and re-layouts  4.22 us

profile of v2, /device:TPU:1, one launch (start us, length us, event | category | flops | bytes accessed | tf_op | source)
XLA Modules:
  0.0 100.0 jit_solution(17410361313909002496)
XLA Ops:
  0.6 0.0 copy-start
  0.6 1.0 %copy-done = s32[128,896]{1,0:T(8,128)S(1)} copy-done((s32[128,896]{1,0:T(8,128)S(1)}, s32[128,896]{1,0:T(8,128)}, u32[]{:S(2)}) %copy-start) | copy-done | bytes 458776
  1.7 0.0 copy-start.1
  1.7 0.9 copy-done.1
  2.6 0.0 copy-start.2
  2.6 0.7 copy-done.2
  3.2 95.2 %shard_map.77 = (bf16[128,896]{1,0:T(8,128)(2,1)S(1)}, bf16[896,512]{1,0:T(8,128)(2,1)S(1)}) custom-call(bf16[128,896]{1,0:T(8,128)(2,1)S(1)} %copy-done.1, bf16[128,8192]{1,0:T(8,128)(2,1)} %refs_1_.1, bf16[896,512]{1,0:T(8,128)(2,1)} %refs_2_.1, s32[128,896]{1,0:T(8,128)S(1)} %copy-done, s32[1,128]{1,0:T(1,128)S(1)} %bitcast.1, ...), custom_call_target="tpu_custom_call" | custom-call | tf_op jit(solution)/shard_map/pallas_call | solution.py:410
  98.4 0.7 copy.10
  99.1 0.9 copy.11
Async XLA Ops:
  0.6 1.0 %copy-start = (s32[128,896]{1,0:T(8,128)S(1)}, s32[128,896]{1,0:T(8,128)}, u32[]{:S(2)}) copy-start(s32[128,896]{1,0:T(8,128)} %refs_3_.1) | copy-start | bytes 1376260
  1.7 0.9 copy-start.1
  2.6 0.7 copy-start.2

commit v3 on v2

--- a/solution.py
+++ b/solution.py
@@ -51,16 +51,21 @@
     return -(-w // 256) * 256
 
 
-def chunk_scratch(Z, Y, R, DB, w):
-    K = Z // 2
+def group_scratch(Z, Y, R, w):
     wide, half = (Y, TR, padded(w)), (2, Y, TR, padded(w) // 2)
     return dict(
         f_own=((R, w), F32), f_s0=((R, w), BF), f_r0=((R, w), BF),
         f_as=(wide, BF), f_ar=(half, BF), f_b=(half, BF), q=((Z,) + wide, BF),
+        b_own=((R, w), F32), b_s0=((R, w), BF), b_r0=((R, w), BF),
+        b_as=(wide, BF), b_ar=(half, BF), b_b=(half, BF), b_q=(wide, BF),
+    )
+
+
+def chunk_scratch(Z, R, DB, w):
+    K = Z // 2
+    return dict(
         xs=((w, DB), BF), xr=((w, DB), BF), wown=((w, DB), F32),
         g=((Z, R, w), F32), rs_s=((2, K, R, w), BF), rs_r=((2, K, R, w), BF),
-        b_own=((R, w), F32), b_s0=((R, w), BF), b_r0=((R, w), BF),
-        b_as=(wide, BF), b_ar=(half, BF), b_b=(half, BF), b_q=(wide, BF),
     )
 
 
@@ -80,19 +85,26 @@
 def kernel(cfg, act_h, cot_h, w_h, mask_h, scale_h, table_h, gin_o, wg_o, *scr):
     Z, Y, R, F, DB, chunks, norm, wscale, order = cfg
     K = Z // 2
-    NC = len(chunks)
+    NG = len(chunks)
     scr = list(scr)
     act_v, table_v, mask_v, scale_v, wbuf, cbuf, step_v, gin_v, lsem, ssem, rsem = scr[:11]
     del scr[:11]
-    ch = []
+    ch, groups = [], []
     at = 0
-    for w in chunks:
-        one = Chunk()
-        one.lo, one.w, one.half = at, w, padded(w) // 2
-        at += w
-        for name in chunk_scratch(Z, Y, R, DB, w):
-            setattr(one, name, scr.pop(0))
-        ch.append(one)
+    for widths in chunks:
+        group = Chunk()
+        group.lo, group.w, group.half, group.parts = at, sum(widths), padded(sum(widths)) // 2, []
+        for name in group_scratch(Z, Y, R, group.w):
+            setattr(group, name, scr.pop(0))
+        groups.append(group)
+        for w in widths:
+            one = Chunk()
+            one.lo, one.w, one.group, one.cols = at, w, group, pl.ds(at - group.lo, w)
+            at += w
+            for name in chunk_scratch(Z, R, DB, w):
+                setattr(one, name, scr.pop(0))
+            group.parts.append(one)
+            ch.append(one)
 
     dp, tn = lax.axis_index("dp"), lax.axis_index("tensor")
     xl, z = lax.div(dp, Z), lax.rem(dp, Z)
@@ -155,7 +167,7 @@
     peers += [dev(xh_=mates(h), y_=yy(n)) for h, n in others] + [dev(z_=zz(k)) for k in range(1, Z)]
     for peer in peers:
         pl.semaphore_signal(barrier, inc=1, device_id=peer, device_id_type=MESH)
-    for k in ch:
+    for k in groups:
         if 2 * k.half > k.w:
             blank = jnp.zeros((Y, TR, 2 * k.half - k.w), BF)
             k.f_as[:, :, pl.ds(k.w, 2 * k.half - k.w)] = blank
@@ -165,7 +177,7 @@
     step_v[...] = jnp.left_shift(jnp.ones_like(exponent), exponent + 3).astype(F32) * 0.125
     act_c.wait()
     table_c.wait()
-    for k in ch:
+    for k in groups:
         value = jnp.dot(act_v[...], table_v[:, pl.ds(k.lo, k.w)], preferred_element_type=F32)
         k.f_own[...] = value
         k.f_s0[...] = value.astype(BF)
@@ -202,8 +214,9 @@
             ch[j - 1].wc.left.wait()
         k.wc = send(w_h.at[rows], wbuf.at[xl, rows], dev(xl_=1 - xl))
 
-    def to_core(k, p):
-        st[p, k, "c"] = [send(getattr(k, p + "s0"), getattr(k, p + "r0"), dev(c_=1 - c))]
+    def to_core(k, p, cols):
+        source, target = getattr(k, p + "s0").at[:, cols], getattr(k, p + "r0").at[:, cols]
+        st.setdefault((p, k, "c"), []).append(send(source, target, dev(c_=1 - c)))
 
     def lanes(k, h):
         return pl.ds(pl.multiple_of(mates(h) * k.half, 128), k.half)
@@ -243,13 +256,13 @@
                 target[pl.ds(y, 1), :, pl.ds(h * k.half, k.half)] = b[h, pl.ds(y, 1)]
 
     def f0(j):
-        to_core(ch[j], "f_")
+        to_core(groups[j], "f_", pl.ds(0, groups[j].w))
 
     def f1(j):
-        to_y(ch[j], "f_")
+        to_y(groups[j], "f_")
 
     def f2(j):
-        k = ch[j]
+        k = groups[j]
         parts = hada(k, "f_")
         step = step_v[pl.ds(y_rows, TR), :][:, 0:1]
         for n in range(2 * Y):
@@ -258,16 +271,16 @@
 
     def ag(j, s):
         k = ch[j]
-        arrived(st["f_", k, "b"] if s == 0 else k.agc)
+        arrived(st["f_", k.group, "b"] if s == 0 else k.agc)
         if s < K:
             last = s == K - 1
             yr, yl = (pl.ds(0, Y // 2), pl.ds(Y // 2, Y // 2)) if last else (pl.ds(0, Y),) * 2
-            cols = pl.ds(0, k.w)
-            right, left = k.q.at[zz(-s), yr, :, cols], k.q.at[zz(s), yl, :, cols]
+            q = k.group.q
+            right, left = q.at[zz(-s), yr, :, k.cols], q.at[zz(s), yl, :, k.cols]
             k.agc = [send(right, right, dev(z_=zz(1))), send(left, left, dev(z_=zz(-1)))]
 
     def wg_dot(k, half, cast):
-        rows = k.q[:, :, :, pl.ds(0, k.w)].reshape(Z * R, k.w)
+        rows = k.group.q[:, :, :, k.cols].reshape(Z * R, k.w)
         cot = cbuf[pl.ds(half, 1)].reshape(Z * R, DB)
         return lax.dot_general(rows, cot, (((0,), (0,)), ((), ())), preferred_element_type=F32).astype(cast)
 
@@ -331,64 +344,60 @@
         total = k.g[z] + k.rs_r[0, K - 1].astype(F32) + k.rs_r[1, K - 1].astype(F32)
         mask = mask_v[:, pl.ds(k.lo, k.w)].astype(F32)
         masked = (mask * total).astype(BF)
-        k.b_own[...] = masked.astype(F32)
-        k.b_s0[...] = masked
-        to_core(k, "b_")
+        k.group.b_own[:, k.cols] = masked.astype(F32)
+        k.group.b_s0[:, k.cols] = masked
+        to_core(k.group, "b_", k.cols)
 
     def b1(j):
-        to_y(ch[j], "b_")
+        to_y(groups[j], "b_")
 
     def b2(j):
-        k = ch[j]
+        k = groups[j]
         parts = hada(k, "b_")
         for n in range(2 * Y):
             k.b_b[n // Y, n % Y] = parts[n].astype(BF)
         back_y(k, "b_", k.b_q)
 
     def b3(j):
-        k = ch[j]
+        k = groups[j]
         arrived(st["b_", k, "b"])
         part = jnp.dot(
             k.b_q[:, :, pl.ds(0, k.w)].reshape(R, k.w), table_v[pl.ds(k.lo, k.w), :], preferred_element_type=F32
         )
         if j > 0:
             part = part + gin_v[...]
-        if j < NC - 1:
+        if j < NG - 1:
             gin_v[...] = part
         else:
             gin_o[...] = (part * norm).astype(BF)
 
     tasks = dict(locals())
-    for name, *args in order(NC, Z):
+    for name, *args in order:
         tasks[name](*args)
     for one in Once.made:
         one.wait()
 
 
-def copies_of(NC, Z, Y):
+def copies_of(chunks, Z, Y):
     cot = (Z - 1) + 5 * Z
-    each = 1 + 2 * (1 + 2 * (2 * Y - 1)) + 4 * (Z // 2) + 1
-    return cot + NC * each
+    group = 1 + 4 * (2 * Y - 1)
+    return cot + len(chunks) * group + sum(map(len, chunks)) * (1 + 4 * (Z // 2) + 2)
 
 
 STEPS = (
-    ('f0', 1), ('cot_z',), ('f0', 0), ('f1', 1), ('f1', 0), ('cot_fwd', 7), ('weights', 0), ('f0', 2), ('f1', 2),
-    ('cot_fwd', 2), ('cot_fwd', 1), ('f2', 0), ('f2', 1), ('f2', 2), ('weights', 1), ('cot_fwd', 6),
-    ('cot_fwd', 5), ('ag', 0, 0), ('cot_in', 2), ('cot_in', 1), ('cot_fwd', 4), ('ag', 1, 0), ('cot_in', 5),
-    ('cot_fwd', 3), ('ag', 0, 1), ('cot_in', 4), ('ag', 2, 0), ('cot_in', 6), ('weights', 2), ('ag', 1, 1),
-    ('cot_in', 3), ('grad', 0, 0), ('cot_in', 7), ('rs', 0, 0), ('grad', 1, 0), ('rs', 1, 0), ('cot_fwd', 0),
-    ('ag', 2, 1), ('grad', 1, 1), ('grad', 0, 1), ('ag', 1, 2), ('rs', 0, 1), ('grad', 0, 2), ('grad', 1, 3),
-    ('grad', 0, 3), ('grad', 1, 2), ('grad', 2, 0), ('rs', 2, 0), ('rs', 1, 1), ('grad', 2, 3), ('cot_in', 0),
-    ('ag', 1, 3), ('rs', 0, 2), ('grad', 2, 1), ('grad', 2, 2), ('grad', 0, 4), ('rs', 2, 1), ('grad', 2, 4),
-    ('ag', 2, 2), ('ag', 1, 4), ('rs', 1, 2), ('wg', 1), ('rs', 0, 3), ('rs', 2, 2), ('rs', 1, 3), ('grad', 1, 4),
-    ('rs', 2, 3), ('ag', 2, 3), ('b0', 0), ('b1', 0), ('b0', 1), ('b1', 1), ('b0', 2), ('ag', 0, 2), ('ag', 2, 4),
-    ('wg', 2), ('b1', 2), ('b2', 0), ('ag', 0, 3), ('b2', 1), ('b2', 2), ('ag', 0, 4), ('wg', 0), ('b3', 0),
-    ('wend', 1), ('b3', 1), ('b3', 2), ('wend', 2), ('wend', 0),
+    ('cot_z',), ('weights', 0), ('f0', 0), ('cot_fwd', 0), ('f1', 0), ('f0', 1), ('weights', 1), ('cot_in', 0),
+    ('f1', 1), ('cot_fwd', 6), ('f2', 0), ('cot_in', 6), ('cot_fwd', 4), ('cot_fwd', 3), ('cot_fwd', 2),
+    ('weights', 2), ('ag', 0, 0), ('f2', 1), ('ag', 1, 0), ('cot_in', 2), ('cot_in', 4), ('ag', 0, 1),
+    ('cot_in', 3), ('cot_fwd', 5), ('grad', 0, 2), ('grad', 0, 0), ('rs', 0, 0), ('grad', 1, 0), ('ag', 1, 1),
+    ('grad', 0, 4), ('rs', 1, 0), ('cot_fwd', 1), ('cot_fwd', 7), ('grad', 2, 0), ('rs', 2, 0), ('ag', 0, 2),
+    ('ag', 2, 0), ('cot_in', 5), ('ag', 1, 2), ('grad', 2, 2), ('grad', 0, 1), ('rs', 0, 1), ('grad', 2, 1),
+    ('cot_in', 1), ('grad', 1, 1), ('rs', 1, 1), ('cot_in', 7), ('rs', 2, 1), ('grad', 0, 3), ('ag', 1, 3),
+    ('ag', 0, 3), ('rs', 0, 2), ('grad', 1, 2), ('rs', 1, 2), ('rs', 2, 2), ('ag', 1, 4), ('ag', 2, 1),
+    ('ag', 0, 4), ('grad', 1, 3), ('rs', 0, 3), ('wg', 0), ('grad', 2, 4), ('rs', 1, 3), ('grad', 2, 3), ('wg', 1),
+    ('grad', 1, 4), ('rs', 2, 3), ('ag', 2, 2), ('b0', 0), ('b0', 1), ('b1', 0), ('b0', 2), ('ag', 2, 3),
+    ('b1', 1), ('ag', 2, 4), ('wg', 2), ('b2', 0), ('wend', 0), ('wend', 1), ('b2', 1), ('b3', 0), ('wend', 2),
+    ('b3', 1),
 )
-
-
-def plan(NC, Z):
-    return STEPS
 
 
 def call(Z, Y, R, F, DB, chunks, norm, wscale, order, args):
@@ -397,15 +406,19 @@
         pltpu.VMEM((2, F, DB), BF), pltpu.VMEM((2, Z, R, DB), BF), pltpu.VMEM((R, R), F32), pltpu.VMEM((R, F), F32),
         pltpu.SemaphoreType.DMA((6,)),
     ]
-    total = copies_of(len(chunks), Z, Y)
+    total = copies_of(chunks, Z, Y)
     scratch += [pltpu.SemaphoreType.DMA((total,)), pltpu.SemaphoreType.DMA((total,))]
-    for w in chunks:
-        scratch += [pltpu.VMEM(*spec) for spec in chunk_scratch(Z, Y, R, DB, w).values()]
+    for widths in chunks:
+        scratch += [pltpu.VMEM(*spec) for spec in group_scratch(Z, Y, R, sum(widths)).values()]
+        for w in widths:
+            scratch += [pltpu.VMEM(*spec) for spec in chunk_scratch(Z, R, DB, w).values()]
     cfg = (Z, Y, R, F, DB, chunks, norm, wscale, order)
     hbm, vmem = pl.BlockSpec(memory_space=pltpu.HBM), pl.BlockSpec(memory_space=pltpu.VMEM)
 
     def run(*refs):
         kernel(cfg, *refs)
+
+    args = [pltpu.with_memory_space_constraint(arg, pltpu.HBM) for arg in args]
 
     return pl.pallas_call(
         run,
@@ -425,7 +438,7 @@
     table = jnp.asarray(np.kron(sylvester(F // 28), paley_table()), BF)
     tokens = R * lax.axis_size("dp")
     return call(
-        8, 8, R, F, DB, (256, 384, 256), 1.0 / math.sqrt(FF), 1.0 / math.sqrt(tokens), plan,
+        8, 8, R, F, DB, ((256, 256), (384,)), 1.0 / math.sqrt(FF), 1.0 / math.sqrt(tokens), STEPS,
         (activations, cotangent, weight, clip_mask, scale_exponent.reshape(1, R), table),
     )
 

time: 100 us -> 95.1 us (0.951)
  Pallas kernels: 95.2 us -> 92.1 us
  local copies, waits for them, and re-layouts: 4.22 us -> 1.61 us
    pallas_call x1, Pallas kernels: 95.2 us -> 92.1 us  [call(): pl.pallas_call(run, out_shape=(jax.ShapeDtypeStruct((R, F), BF), jax.Shap...]
    unnamed x8 -> x2, local copies, waits for them, and re-layouts: 4.22 us -> 1.61 us
where the time goes in v3:
time: 95.1 us; the launch traced here: 94.4 us
  Pallas kernels  92.1 us (97%)
  local copies, waits for them, and re-layouts  1.61 us (2%)
    pallas_call x1, Pallas kernels, call(): pl.pallas_call(run, out_shape=(jax.ShapeDtypeStruct((R, F), BF), jax.Shap...  92.1 us

profile of v3, /device:TPU:1, one launch (start us, length us, event | category | flops | bytes accessed | tf_op | source)
XLA Modules:
  0.0 94.4 jit_solution(14144729403580297023)
XLA Ops:
  0.6 92.1 %shard_map.77 = (bf16[128,896]{1,0:T(8,128)(2,1)S(1)}, bf16[896,512]{1,0:T(8,128)(2,1)S(1)}) custom-call(bf16[128,896]{1,0:T(8,128)(2,1)} %refs_0_.1, bf16[128,8192]{1,0:T(8,128)(2,1)} %refs_1_.1, bf16[896,512]{1,0:T(8,128)(2,1)} %refs_2_.1, s32[128,896]{1,0:T(8,128)} %refs_3_.1, s32[1,128]{1,0:T(1,128)} %bitcast.1, bf16[896,896]{1,0:T(8,128)(2,1)} %constant.2.clone.refs_5_), custom_call_target="tpu_custom_call" | custom-call | tf_op jit(solution)/shard_map/pallas_call | solution.py:423
  92.7 0.7 copy.10
  93.4 0.9 copy.11

commit v4 on v3

--- a/solution.py
+++ b/solution.py
@@ -385,18 +385,17 @@
 
 
 STEPS = (
-    ('cot_z',), ('weights', 0), ('f0', 0), ('cot_fwd', 0), ('f1', 0), ('f0', 1), ('weights', 1), ('cot_in', 0),
-    ('f1', 1), ('cot_fwd', 6), ('f2', 0), ('cot_in', 6), ('cot_fwd', 4), ('cot_fwd', 3), ('cot_fwd', 2),
-    ('weights', 2), ('ag', 0, 0), ('f2', 1), ('ag', 1, 0), ('cot_in', 2), ('cot_in', 4), ('ag', 0, 1),
-    ('cot_in', 3), ('cot_fwd', 5), ('grad', 0, 2), ('grad', 0, 0), ('rs', 0, 0), ('grad', 1, 0), ('ag', 1, 1),
-    ('grad', 0, 4), ('rs', 1, 0), ('cot_fwd', 1), ('cot_fwd', 7), ('grad', 2, 0), ('rs', 2, 0), ('ag', 0, 2),
-    ('ag', 2, 0), ('cot_in', 5), ('ag', 1, 2), ('grad', 2, 2), ('grad', 0, 1), ('rs', 0, 1), ('grad', 2, 1),
-    ('cot_in', 1), ('grad', 1, 1), ('rs', 1, 1), ('cot_in', 7), ('rs', 2, 1), ('grad', 0, 3), ('ag', 1, 3),
-    ('ag', 0, 3), ('rs', 0, 2), ('grad', 1, 2), ('rs', 1, 2), ('rs', 2, 2), ('ag', 1, 4), ('ag', 2, 1),
-    ('ag', 0, 4), ('grad', 1, 3), ('rs', 0, 3), ('wg', 0), ('grad', 2, 4), ('rs', 1, 3), ('grad', 2, 3), ('wg', 1),
-    ('grad', 1, 4), ('rs', 2, 3), ('ag', 2, 2), ('b0', 0), ('b0', 1), ('b1', 0), ('b0', 2), ('ag', 2, 3),
-    ('b1', 1), ('ag', 2, 4), ('wg', 2), ('b2', 0), ('wend', 0), ('wend', 1), ('b2', 1), ('b3', 0), ('wend', 2),
-    ('b3', 1),
+    ('f0', 0), ('weights', 0), ('cot_z',), ('cot_fwd', 0), ('f0', 1), ('f1', 0), ('weights', 1), ('f1', 1),
+    ('f2', 0), ('cot_fwd', 4), ('f2', 1), ('weights', 2), ('ag', 0, 0), ('cot_fwd', 2), ('cot_fwd', 5),
+    ('cot_fwd', 3), ('cot_fwd', 6), ('cot_in', 0), ('ag', 1, 0), ('ag', 0, 1), ('ag', 2, 0), ('cot_in', 4),
+    ('grad', 0, 0), ('ag', 1, 1), ('grad', 1, 0), ('rs', 1, 0), ('cot_fwd', 1), ('grad', 2, 0), ('cot_fwd', 7),
+    ('ag', 0, 2), ('cot_in', 2), ('rs', 2, 0), ('rs', 0, 0), ('cot_in', 6), ('cot_in', 3), ('cot_in', 5),
+    ('ag', 2, 1), ('grad', 2, 1), ('grad', 0, 4), ('grad', 0, 1), ('ag', 1, 2), ('grad', 1, 2), ('cot_in', 1),
+    ('grad', 1, 1), ('rs', 1, 1), ('rs', 0, 1), ('cot_in', 7), ('grad', 1, 4), ('ag', 0, 3), ('grad', 1, 3),
+    ('rs', 2, 1), ('grad', 0, 2), ('grad', 0, 3), ('ag', 1, 3), ('grad', 2, 2), ('ag', 2, 2), ('grad', 2, 4),
+    ('rs', 1, 2), ('ag', 0, 4), ('wg', 0), ('rs', 0, 2), ('rs', 2, 2), ('rs', 1, 3), ('ag', 1, 4), ('rs', 0, 3),
+    ('grad', 2, 3), ('rs', 2, 3), ('ag', 2, 3), ('wg', 1), ('b0', 1), ('b0', 0), ('b1', 0), ('b0', 2), ('wend', 0),
+    ('b1', 1), ('ag', 2, 4), ('wg', 2), ('b2', 0), ('wend', 1), ('b2', 1), ('b3', 0), ('wend', 2), ('b3', 1),
 )
 
 

time: 95.1 us -> 97.4 us (1.024)
  Pallas kernels: 92.1 us -> 95.1 us
    pallas_call x1, Pallas kernels: 92.1 us -> 95.1 us  [call(): pl.pallas_call(run, out_shape=(jax.ShapeDtypeStruct((R, F), BF), jax.Shap...]
where the time goes in v4:
time: 97.4 us; the launch traced here: 97.3 us
  Pallas kernels  95.1 us (98%)
  local copies, waits for them, and re-layouts  1.61 us (2%)
    pallas_call x1, Pallas kernels, call(): pl.pallas_call(run, out_shape=(jax.ShapeDtypeStruct((R, F), BF), jax.Shap...  95.1 us

profile of v4, /device:TPU:1, one launch (start us, length us, event | category | flops | bytes accessed | tf_op | source)
XLA Modules:
  0.0 97.3 jit_solution(12507530137208798234)
XLA Ops:
  0.6 95.1 %shard_map.77 = (bf16[128,896]{1,0:T(8,128)(2,1)S(1)}, bf16[896,512]{1,0:T(8,128)(2,1)S(1)}) custom-call(bf16[128,896]{1,0:T(8,128)(2,1)} %refs_0_.1, bf16[128,8192]{1,0:T(8,128)(2,1)} %refs_1_.1, bf16[896,512]{1,0:T(8,128)(2,1)} %refs_2_.1, s32[128,896]{1,0:T(8,128)} %refs_3_.1, s32[1,128]{1,0:T(1,128)} %bitcast.1, bf16[896,896]{1,0:T(8,128)(2,1)} %constant.2.clone.refs_5_), custom_call_target="tpu_custom_call" | custom-call | tf_op jit(solution)/shard_map/pallas_call | solution.py:422
  95.7 0.7 copy.10
  96.4 0.9 copy.11
